TPU v7x, 32 devices: a whole 2x2x4 slice. The times are simulated.
32 devices in a mesh: row: 8 (over y, x, core), col: 4 (over z).
Axes of the slice: x: 2, y: 2, z: 4, core: 2. Of those that a mesh axis runs over, the one named last changes fastest.
Arguments:
- saved_factor: float32 [4096, 4096], P('row', 'col'), may hold values from -1 to 3, as said below
- cotangent: float32 [4096, 4096], P('row', 'col'), may hold values from -6 to 6
Outputs:
- adjoint: float32 [4096, 4096], P('row', 'col')
Inputs may be any that keep to these rules, and one draw needn't show every extreme that they name: `saved_factor`: entry (i, j) is zero where j > i + 4096 - 3 * 512, and 1 or more where j = i + 4096 - 3 * 512.
All inputs are finite; a program needn't handle non-finite values.
Results may differ from a plain program's by a relative error of at most 0.0001.
Values sent between devices are 32-bit elements; how exact they have to be, the bound alone decides.
No kernel may reach another device: no remote copies, remote signals or barrier semaphores. Data moves between devices by JAX's collectives and lax.ppermute only.
A program may use at most 128 MiB of HBM per device.

v0:
```python
import jax
import jax.numpy as jnp
from jax import lax
from jax.sharding import PartitionSpec as P

NB = 512
NP = 3


precise = lax.Precision.HIGHEST


def from_root(shard, axis, root):
    mine = lax.axis_index(axis) == root
    return lax.psum(jnp.where(mine, shard, jnp.zeros_like(shard)), axis)


def matmul(left_side, right_side):
    return jnp.dot(left_side, right_side, precision=precise, preferred_element_type=jnp.float32)


def inner_rows(left_side, right_side):
    return lax.dot_general(
        left_side,
        right_side,
        (((0,), (0,)), ((), ())),
        precision=precise,
        preferred_element_type=jnp.float32,
    )


def lower_half(matrix):
    return jnp.tril(matrix) - 0.5 * jnp.diag(jnp.diag(matrix))


def adjoint_of(diag_factor, diag_cot, diag_sum, inverse):
    diag_grad = jnp.tril(diag_cot) - jnp.tril(diag_sum)
    return lower_half(
        matmul(matmul(inverse.T, lower_half(matmul(diag_factor.T, diag_grad))), inverse)
    )


def fetch(saved_factor, cotangent, row_start, col_start, rows_dev, cols_dev, col_count):
    owner_row = row_start // rows_dev
    owner_col = col_start // cols_dev
    row_shift = row_start % rows_dev
    col_shift = col_start % cols_dev
    blocks = jnp.stack(
        [
            saved_factor[row_shift : row_shift + NB, col_shift : col_shift + NB],
            cotangent[row_shift : row_shift + NB, col_shift : col_shift + NB],
        ]
    )
    blocks = from_root(blocks, ("row", "col"), owner_row * col_count + owner_col)
    strip_rows = from_root(saved_factor, "row", owner_row)
    return (blocks, strip_rows)


def shards(saved_factor, cotangent):
    rows_dev, cols_dev = saved_factor.shape
    row_count = lax.axis_size("row")
    col_count = lax.axis_size("col")
    full_order = rows_dev * row_count
    this_row = lax.axis_index("row")
    this_col = lax.axis_index("col")
    row_ids = this_row * rows_dev + jnp.arange(rows_dev, dtype=jnp.int32)
    col_ids = this_col * cols_dev + jnp.arange(cols_dev, dtype=jnp.int32)
    row_starts = [(NP - 1 - number) * NB for number in range(NP)]
    col_starts = [full_order - (number + 1) * NB for number in range(NP)]
    identity = jnp.eye(NB, dtype=saved_factor.dtype)
    running = cotangent
    for number in range(NP):
        row_start = row_starts[number]
        row_end = row_start + NB
        col_start = col_starts[number]
        blocks, strip_rows = fetch(
            saved_factor, cotangent, row_start, col_start, rows_dev, cols_dev, col_count
        )
        owner_row = row_start // rows_dev
        owner_col = col_start // cols_dev
        row_shift = row_start % rows_dev
        col_shift = col_start % cols_dev
        diag_factor = blocks[0]
        diag_cot = blocks[1]
        inverse = lax.linalg.triangular_solve(diag_factor, identity, left_side=True, lower=True)
        below_mask = (row_ids >= row_end)[:, None]
        left_mask = (col_ids < col_start)[None, :]
        owns_col = this_col == owner_col
        owns_row = this_row == owner_row
        panel_cot = jnp.where(below_mask, running[:, col_shift : col_shift + NB], 0.0)
        panel_factor = jnp.where(below_mask, saved_factor[:, col_shift : col_shift + NB], 0.0)
        arrived = from_root(jnp.stack([matmul(panel_cot, inverse), panel_factor]), "col", owner_col)
        solved = arrived[0]
        below_factor = arrived[1]
        running = running.at[:, col_shift : col_shift + NB].set(
            jnp.where(owns_col & below_mask, solved, running[:, col_shift : col_shift + NB])
        )
        left_strip = jnp.where(left_mask, strip_rows, 0.0)
        running = running - matmul(solved, left_strip)
        left_block = jnp.where(below_mask & left_mask, saved_factor, 0.0)
        strip_part = inner_rows(solved, left_block)
        diag_part = inner_rows(solved, below_factor)
        old_strip = running
        strip_sum, diag_sum = lax.psum((strip_part, diag_part), "row")
        diag_adj = adjoint_of(diag_factor, diag_cot, diag_sum, inverse)
        new_strip = old_strip - strip_sum - matmul(diag_adj + diag_adj.T, left_strip)
        running = running.at[row_shift : row_shift + NB, :].set(
            jnp.where(owns_row, new_strip, old_strip)
        )
        running = running.at[row_shift : row_shift + NB, col_shift : col_shift + NB].set(
            jnp.where(
                owns_row & owns_col,
                diag_adj,
                running[row_shift : row_shift + NB, col_shift : col_shift + NB],
            )
        )
    return running


def solution(mesh):
    placed = (P("row", "col"), P("row", "col"))
    return jax.shard_map(
        shards, mesh=mesh, in_specs=placed, out_specs=P("row", "col"), check_vma=False
    )
```

profile of v0, /device:TPU:1, one launch (start us, length us, event | category | flops | bytes accessed | tf_op | source)
XLA Modules:
  0.0 925.4 jit_solution(4327342682940749815)
XLA Ops:
  6.5 3.1 copy.52
  9.7 2.8 slice_bitcast_fusion.15
  12.5 2.0 slice_bitcast_fusion.19
  16.1 2.6 fusion.22
  18.9 158.3 %all-reduce.18.cloned.1.call-done = (f32[2,512,512]{2,1,0:T(8,128)}, f32[2,512,512]{2,1,0:T(8,128)}, f32[2,512,512]{2,1,0:T(8,128)}) async-done(((f32[2,512,512]{2,1,0:T(8,128)}, f32[2,512,512]{2,1,0:T(8,128)}, f32[2,512,512]{2,1,0:T(8,128)}), (f32[2,512,512]{2,1,0:T(8,128)}, f32[2,512,512]{2,1,0:T(8,128)}, f32[2,512,512]{2,1,0:T(8,128)})) %all-reduce.18.cloned.1.call-update) | async-done | bytes 6291472 | tf_op jit(solution)/shard_map/psum | solution.py:15
  177.3 2.3 fusion.68
  179.6 11.7 %while.18 = (s32[]{:T(128)}, f32[512,512]{1,0:T(8,128)}, s32[4,2]{0,1:T(2,128)S(1)}, f32[4,128,128]{2,1,0:T(8,128)S(1)}, s32[]{:T(128)}) while((s32[]{:T(128)}, f32[512,512]{1,0:T(8,128)}, s32[4,2]{0,1:T(2,128)S(1)}, f32[4,128,128]{2,1,0:T(8,128)S(1)}, s32[]{:T(128)}) %tuple.103), condition=%wide.while_cond.9, body=%wide.while_body.9.sunk | while | flops 2 | bytes 131189 | solution.py:85
  180.3 2.3 bitcast_dynamic-update-slice_fusion.6
  183.2 2.3 bitcast_dynamic-update-slice_fusion.6
  186.2 2.3 bitcast_dynamic-update-slice_fusion.6
  189.1 2.2 bitcast_dynamic-update-slice_fusion.6
  192.0 40.1 %custom-call.17 = f32[4,128,128]{1,2,0:T(8,128)S(1)} custom-call(f32[4,128,128]{2,1,0:T(8,128)} %copy-done.52), custom_call_target="InvertDiagBlocksLowerTriangular" | custom-call | tf_op jit(solution)/shard_map/triangular_solve/custom-call.1 | solution.py:85
  238.3 3.2 convolution_bitcast_fusion.2
  243.7 3.1 broadcast_select_fusion.2
  247.9 82.3 %all-reduce.12.cloned.1.call-done = f32[2,512,512]{2,1,0:T(8,128)} async-done(((f32[2,512,512]{2,1,0:T(8,128)}), f32[2,512,512]{2,1,0:T(8,128)}) %all-reduce.12.cloned.1.call-update) | async-done | bytes 2097168 | tf_op jit(solution)/shard_map/psum | solution.py:15
  330.2 4.5 fusion.43
  334.7 5.1 fusion.4
  340.1 11.7 %while.19 = (s32[]{:T(128)}, f32[512,512]{1,0:T(8,128)}, s32[4,2]{0,1:T(2,128)S(1)}, f32[4,128,128]{2,1,0:T(8,128)S(1)}, s32[]{:T(128)}) while((s32[]{:T(128)}, f32[512,512]{1,0:T(8,128)}, s32[4,2]{0,1:T(2,128)S(1)}, f32[4,128,128]{2,1,0:T(8,128)S(1)}, s32[]{:T(128)}) %tuple.130), condition=%wide.while_cond.9.clone, body=%wide.while_body.9.clone.sunk | while | flops 2 | bytes 131189 | solution.py:85
  340.7 2.3 bitcast_dynamic-update-slice_fusion.7
  343.7 2.3 bitcast_dynamic-update-slice_fusion.7
  346.7 2.3 bitcast_dynamic-update-slice_fusion.7
  349.6 2.2 bitcast_dynamic-update-slice_fusion.7
  351.8 39.9 %custom-call.18 = f32[4,128,128]{1,2,0:T(8,128)} custom-call(f32[4,128,128]{2,1,0:T(8,128)S(1)} %get-tuple-element.159), custom_call_target="InvertDiagBlocksLowerTriangular" | custom-call | tf_op jit(solution)/shard_map/triangular_solve/custom-call.1 | solution.py:85
  400.4 2.4 select_dynamic-update-slice_fusion.1
  402.9 29.2 %all-reduce.24.cloned.1.call-done = (f32[512,1024]{1,0:T(8,128)}, f32[512,512]{1,0:T(8,128)}, f32[512,1024]{1,0:T(8,128)}) async-done(((f32[512,1024]{1,0:T(8,128)}, f32[512,512]{1,0:T(8,128)}, f32[512,1024]{1,0:T(8,128)}), (f32[512,1024]{1,0:T(8,128)}, f32[512,512]{1,0:T(8,128)}, f32[512,1024]{1,0:T(8,128)})) %all-reduce.24.cloned.1.call-update) | async-done | bytes 5242896 | tf_op jit(solution)/shard_map/psum | solution.py:15
  432.1 3.7 fusion.46
  435.8 4.5 gather_fusion
  440.4 3.3 fusion.71
  446.9 4.9 gather_fusion.1
  451.8 5.7 fusion.17
  457.6 6.2 subtract_select_fusion.2
  463.8 2.5 fusion.42
  466.4 3.2 convolution_bitcast_fusion.1
  471.9 2.3 fusion.57
  474.3 83.8 %all-reduce.14.cloned.1.call-done = f32[2,512,512]{2,1,0:T(8,128)} async-done(((f32[2,512,512]{2,1,0:T(8,128)}), f32[2,512,512]{2,1,0:T(8,128)}) %all-reduce.14.cloned.1.call-update) | async-done | bytes 2097168 | tf_op jit(solution)/shard_map/psum | solution.py:15
  558.1 4.5 fusion.37
  562.6 5.1 fusion.2
  568.5 14.0 %while.20 = (s32[]{:T(128)}, f32[512,512]{1,0:T(8,128)}, s32[4,2]{0,1:T(2,128)S(1)}, f32[4,128,128]{2,1,0:T(8,128)}, s32[]{:T(128)}) while((s32[]{:T(128)}, f32[512,512]{1,0:T(8,128)}, s32[4,2]{0,1:T(2,128)S(1)}, f32[4,128,128]{2,1,0:T(8,128)}, s32[]{:T(128)}) %tuple.131), condition=%wide.while_cond.9.clone.1, body=%wide.while_body.9.clone.1.sunk | while | flops 2 | bytes 132205 | solution.py:85
  569.3 2.9 bitcast_dynamic-update-slice_fusion.8
  572.8 2.9 bitcast_dynamic-update-slice_fusion.8
  576.2 2.9 bitcast_dynamic-update-slice_fusion.8
  579.7 2.8 bitcast_dynamic-update-slice_fusion.8
  582.5 40.7 %custom-call.19 = f32[4,128,128]{1,2,0:T(8,128)} custom-call(f32[4,128,128]{2,1,0:T(8,128)} %get-tuple-element.160), custom_call_target="InvertDiagBlocksLowerTriangular" | custom-call | tf_op jit(solution)/shard_map/triangular_solve/custom-call.1 | solution.py:85
  632.0 3.0 fusion.29
  635.0 25.0 %all-reduce.22.cloned.1.call-done = (f32[512,1024]{1,0:T(8,128)}, f32[512,512]{1,0:T(8,128)}, f32[512,1024]{1,0:T(8,128)}) async-done(((f32[512,1024]{1,0:T(8,128)}, f32[512,512]{1,0:T(8,128)}, f32[512,1024]{1,0:T(8,128)}), (f32[512,1024]{1,0:T(8,128)}, f32[512,512]{1,0:T(8,128)}, f32[512,1024]{1,0:T(8,128)})) %all-reduce.22.cloned.1.call-update) | async-done | bytes 5242896 | tf_op jit(solution)/shard_map/psum | solution.py:15
  660.1 3.8 fusion.40
  663.8 4.5 gather_fusion.2
  668.4 3.2 fusion.76
  671.6 1.9 fusion.191
  674.8 4.7 gather_fusion.3
  679.5 5.7 fusion.13
  685.3 5.5 subtract_select_fusion.1
  693.4 1.9 convolution_bitcast_fusion
  697.4 86.4 %all-reduce.16.cloned.1.call-done = f32[2,512,512]{2,1,0:T(8,128)} async-done(((f32[2,512,512]{2,1,0:T(8,128)}), f32[2,512,512]{2,1,0:T(8,128)}) %all-reduce.16.cloned.1.call-update) | async-done | bytes 2097168 | tf_op jit(solution)/shard_map/psum | solution.py:15
  783.8 4.5 fusion.32
  788.3 5.1 fusion
  796.4 89.0 %all-reduce.20.cloned.1.call-done = (f32[512,1024]{1,0:T(8,128)}, f32[512,512]{1,0:T(8,128)}, f32[512,1024]{1,0:T(8,128)}) async-done(((f32[512,1024]{1,0:T(8,128)}, f32[512,512]{1,0:T(8,128)}, f32[512,1024]{1,0:T(8,128)}), (f32[512,1024]{1,0:T(8,128)}, f32[512,512]{1,0:T(8,128)}, f32[512,1024]{1,0:T(8,128)})) %all-reduce.20.cloned.1.call-update) | async-done | bytes 5242896 | tf_op jit(solution)/shard_map/psum | solution.py:15
  885.5 3.8 fusion.35
  889.2 4.7 gather_fusion.4
  894.0 3.2 fusion.81
  900.4 4.5 gather_fusion.5
  904.9 5.7 fusion.9
  910.7 5.2 subtract_select_fusion
  915.9 2.5 fusion.31
  (193 shorter events, 55.5 us)
Async XLA Ops:
  6.5 170.7 %all-reduce.18.cloned.1.call-start = ((), (), s32[]{:S(2)}) async-start(), calls=%async_computation.3 | async-start | bytes 12582912 | tf_op jit(solution)/shard_map/psum | solution.py:15
  9.7 2.8 copy-start
  14.5 1.6 copy-start.29
  18.7 311.4 %all-reduce.12.cloned.1.call-start = ((), (), s32[]{:S(2)}) async-start(), calls=%async_computation | async-start | bytes 4194304 | tf_op jit(solution)/shard_map/psum | solution.py:15
  18.9 378.7 %copy-start.3 = (f32[512,512]{1,0:T(8,128)}, f32[512,512]{1,0:T(8,128)S(1)}, u32[]{:S(2)}) copy-start(f32[512,512]{1,0:T(8,128)S(1)} %fusion.107) | copy-start | bytes 3145732
  191.3 0.7 copy-start.52
  232.6 5.7 copy-start.13
  234.3 7.2 copy-start.24
  236.2 5.4 copy-start.33
  237.9 3.7 copy-start.20
  238.3 3.3 copy-start.46
  243.1 188.9 %all-reduce.24.cloned.1.call-start = ((), (), s32[]{:S(2)}) async-start(), calls=%async_computation.6 | async-start | bytes 10485760 | tf_op jit(solution)/shard_map/psum | solution.py:15
  243.7 3.1 copy-start.17
  330.2 4.5 copy-start.5
  339.8 218.3 %all-reduce.14.cloned.1.call-start = ((), (), s32[]{:S(2)}) async-start(), calls=%async_computation.1 | async-start | bytes 4194304 | tf_op jit(solution)/shard_map/psum | solution.py:15
  391.7 5.4 copy-start.51
  394.3 6.1 copy-start.6
  395.7 3.6 copy-start.21
  397.6 1.7 copy-start.30
  440.3 3.3 copy-start.14
  440.4 3.3 copy-start.25
  440.4 3.3 copy-start.34
  440.4 3.3 copy-start.47
  451.8 5.8 copy-start.7
  451.8 5.8 copy-start.40
  451.8 5.8 copy-start.41
  463.8 2.5 copy-start.22
  463.8 2.5 copy-start.31
  463.8 2.5 copy-start.44
  466.4 3.2 copy-start.19
  471.3 188.8 %all-reduce.22.cloned.1.call-start = ((), (), s32[]{:S(2)}) async-start(), calls=%async_computation.5 | async-start | bytes 10485760 | tf_op jit(solution)/shard_map/psum | solution.py:15
  558.1 4.5 copy-start.8
  567.7 55.5 %copy-start.4 = (f32[512,512]{1,0:T(8,128)S(1)}, f32[512,512]{1,0:T(8,128)}, u32[]{:S(2)}) copy-start(f32[512,512]{1,0:T(8,128)} %copy-done.3) | copy-start | bytes 3145732
  567.7 216.0 %all-reduce.16.cloned.1.call-start = ((), (), s32[]{:S(2)}) async-start(), calls=%async_computation.2 | async-start | bytes 4194304 | tf_op jit(solution)/shard_map/psum | solution.py:15
  623.3 5.5 copy-start.50
  624.6 6.3 copy-start.15
  625.9 6.1 copy-start.9
  627.3 3.6 copy-start.26
  629.2 1.7 copy-start.35
  668.4 3.2 copy-start.23
  668.4 3.2 copy-start.32
  668.4 3.2 copy-start.45
  679.5 5.8 copy-start.10
  679.5 5.8 copy-start.38
  679.5 5.8 copy-start.39
  690.8 2.6 copy-start.16
  690.8 2.6 copy-start.27
  690.8 2.6 copy-start.36
  690.8 2.6 copy-start.48
  692.0 1.4 copy-start.1
  693.4 1.9 copy-start.18
  696.9 188.5 %all-reduce.20.cloned.1.call-start = ((), (), s32[]{:S(2)}) async-start(), calls=%async_computation.4 | async-start | bytes 10485760 | tf_op jit(solution)/shard_map/psum | solution.py:15
  783.8 4.5 copy-start.11
  793.4 1.6 copy-start.2
  893.9 3.2 copy-start.28
  893.9 3.2 copy-start.37
  893.9 3.2 copy-start.49
  904.9 5.8 copy-start.12
  904.9 5.8 copy-start.42
  904.9 5.8 copy-start.43
Sparse Core Ops, SparseCore 0:
  18.9 158.3 all-reduce.17
  243.3 86.8 all-reduce.11
  339.9 92.0 all-reduce.23
  471.4 86.6 all-reduce.13
  567.9 92.1 all-reduce.21
  697.0 86.6 all-reduce.15
  793.5 91.8 all-reduce.19
where the time goes:
time: 934 us; the launch traced here: 925 us
  waiting for transfers between devices  554 us (59%)
  other arithmetic  154 us (16%)
  matrix products  121 us (13%)
  local copies, waits for them, and re-layouts  79.5 us (9%)
  between operations  14.8 us (2%)
    psum x7, waiting for transfers between devices, from_root(): return lax.psum(jnp.where(mine, shard, jnp.zeros_like(shard)), axis)  554 us
    another operation x7, other arithmetic, shards(): lax.linalg.triangular_solve(diag_factor, identity, left_side=True, lower=...  127 us
    dot_general x18, matrix products, matmul(): jnp.dot(left_side, right_side, precision=precise, preferred_element_type=...  69 us
    another operation x40, local copies, waits for them, and re-layouts, shards(): lax.linalg.triangular_solve(diag_factor, identity, left_side=True, lower=...  37.9 us
    dot_general x6, matrix products, inner_rows(): lax.dot_general(left_side, right_side, (((0,), (0,)), ((), ())), precisio...  28.8 us
    gather x6, local copies, waits for them, and re-layouts, lower_half(): return jnp.tril(matrix) - 0.5 * jnp.diag(jnp.diag(matrix))  27.9 us
    another operation x21, matrix products, shards(): lax.linalg.triangular_solve(diag_factor, identity, left_side=True, lower=...  23.3 us
  transfers between devices with their start and end apart: 7, of which 7 were waited for; matrix products, arithmetic and copies ran while one was open for 15% of the time, Pallas kernels for 0%

commit v1 on v0

v1 whole, which is shorter than its diff:
```python
import functools

import jax
import jax.numpy as jnp
from jax import lax
from jax.experimental import pallas as pl
from jax.experimental.pallas import tpu as pltpu
from jax.sharding import PartitionSpec as P

NB = 512
NP = 3
HALF = NB // 2
BASE = 16
TILE = 128

fine = lax.Precision.HIGHEST
good = lax.Precision.HIGH


def mm(left, right, precision=good):
    return jnp.dot(left, right, precision=precision, preferred_element_type=jnp.float32)


def mm_t(left, right, precision=good):
    return lax.dot_general(
        left, right, (((0,), (0,)), ((), ())), precision=precision, preferred_element_type=jnp.float32
    )


def lower_half(matrix):
    return jnp.tril(matrix) - 0.5 * jnp.diag(jnp.diag(matrix))


def fine_dot(left, right):
    return jnp.dot(left, right, precision=fine, preferred_element_type=jnp.float32)


def inverse_kernel(d_ref, x_ref, tiles, base):
    for t in range(NB // TILE):
        span = pl.ds(t * TILE, TILE)
        tiles[span, :] = d_ref[span, span]
    blocks = NB // BASE
    lane = lax.broadcasted_iota(jnp.int32, (blocks, TILE), 1)
    first = lax.rem(lax.broadcasted_iota(jnp.int32, (blocks, TILE), 0), TILE // BASE) * BASE
    place = lane - first
    solved = []
    for i in range(BASE):
        row = tiles[pl.ds(i, blocks, stride=BASE), :]
        acc = jnp.where(place == i, 1.0, 0.0)
        for k in range(i):
            factor = jnp.sum(jnp.where(place == k, row, 0.0), axis=1, keepdims=True)
            acc = acc - factor * solved[k]
        pivot = jnp.sum(jnp.where(place == i, row, 0.0), axis=1, keepdims=True)
        solved.append(acc / pivot)
        base[pl.ds(i, blocks, stride=BASE), :] = solved[i]
    rows = lax.broadcasted_iota(jnp.int32, (HALF, HALF), 0)
    cols = lax.broadcasted_iota(jnp.int32, (HALF, HALF), 1)
    empty = jnp.zeros((TILE, TILE), jnp.float32)
    corners = []
    for t in range(2):
        top = jnp.concatenate([base[pl.ds(t * HALF, TILE), :], empty], axis=1)
        bottom = jnp.concatenate([empty, base[pl.ds(t * HALF + TILE, TILE), :]], axis=1)
        corners.append(jnp.concatenate([top, bottom], axis=0))
    size = BASE
    while size < HALF:
        below = (rows // (2 * size) == cols // (2 * size)) & (rows // size != cols // size) & (rows > cols)
        for t in range(2):
            span = pl.ds(t * HALF, HALF)
            part = jnp.where(below, d_ref[span, span], 0.0)
            corners[t] = corners[t] - fine_dot(fine_dot(corners[t], part), corners[t])
        size *= 2
    top, bottom = pl.ds(0, HALF), pl.ds(HALF, HALF)
    x_ref[top, top] = corners[0]
    x_ref[top, bottom] = jnp.zeros((HALF, HALF), jnp.float32)
    x_ref[bottom, top] = -fine_dot(fine_dot(corners[1], d_ref[bottom, top]), corners[0])
    x_ref[bottom, bottom] = corners[1]


def invert(matrix):
    return pl.pallas_call(
        inverse_kernel,
        out_shape=jax.ShapeDtypeStruct((NB, NB), jnp.float32),
        in_specs=[pl.BlockSpec(memory_space=pltpu.VMEM)],
        out_specs=pl.BlockSpec(memory_space=pltpu.VMEM),
        scratch_shapes=[pltpu.VMEM((NB, TILE), jnp.float32), pltpu.VMEM((NB, TILE), jnp.float32)],
        compiler_params=pltpu.CompilerParams(vmem_limit_bytes=32 * 1024 * 1024),
        cost_estimate=pl.CostEstimate(flops=20 * 2 * HALF**3 * 6, bytes_accessed=2 * 4 * NB * NB, transcendentals=0),
        name="invert",
    )(matrix)


class Grid:
    def __init__(self):
        self.row_count = lax.axis_size("row")
        self.col_count = lax.axis_size("col")
        self.row = lax.axis_index("row")
        self.col = lax.axis_index("col")
        self.odd = self.row % 2 == 1
        self.paired = self.row_count == 8

    def send(self, value, pairs):
        count = self.col_count
        flat = [(a[0] * count + a[1], b[0] * count + b[1]) for a, b in pairs]
        return lax.ppermute(value, ("row", "col"), flat)

    def within(self, value, moves, planes):
        return self.send(value, [((a, c), (b, c)) for c in planes for a, b in moves])

    def down(self, value, rows, planes):
        return self.send(value, [((r, c), (r, c - 1)) for c in planes for r in rows])

    def is_row(self, *rows):
        return functools.reduce(jnp.logical_or, [self.row == r for r in rows])


def spread(grid, carry, root):
    planes = range(grid.col_count)
    if not grid.paired:
        bit = 1
        while bit < grid.row_count:
            carry = carry + grid.within(carry, [(root ^ m, root ^ m ^ bit) for m in range(bit)], planes)
            bit *= 2
        return carry
    base = root & ~1
    for moves in (((0, 4), (1, 3)), ((4, 6), (3, 7), (1, 5), (0, 2))):
        carry = carry + grid.within(carry, [(a ^ base, b ^ base) for a, b in moves], planes)
    other = grid.within(carry, [(r, r ^ 1) for r in range(grid.row_count)], planes)
    upper = jnp.where(grid.odd, other, carry)
    lower = jnp.where(grid.odd, carry, other)
    return jnp.concatenate([upper, lower], axis=0)


def gather_sum(grid, part, roots):
    if not roots:
        return jnp.zeros_like(part)
    chosen = functools.reduce(
        jnp.logical_or, [(grid.col == c) & (grid.row == root) for c, root in roots.items()]
    )

    def pairs(moves):
        return [((a ^ (root & ~1), c), (b ^ (root & ~1), c)) for c, root in roots.items() for a, b in moves]

    if not grid.paired:
        bit = grid.row_count // 2
        while bit:
            part = part + grid.send(
                part,
                [((root ^ m ^ bit, c), (root ^ m, c)) for c, root in roots.items() for m in range(bit)],
            )
            bit //= 2
        return jnp.where(chosen, part, 0.0)
    half = part.shape[0] // 2
    upper, lower = part[:half], part[half:]
    swapped = grid.send(
        jnp.where(grid.odd, upper, lower),
        [((r, c), (r ^ 1, c)) for c in roots for r in range(grid.row_count)],
    )
    carry = jnp.where(grid.odd, lower, upper) + swapped
    carry = carry + grid.send(carry, pairs(((6, 4), (7, 3), (5, 1), (2, 0))))
    carry = carry + grid.send(carry, pairs(((4, 0), (3, 1))))
    other = grid.send(carry, [((root ^ 1, c), (root, c)) for c, root in roots.items()])
    carry = jnp.where(chosen, carry, 0.0)
    return jnp.concatenate(
        [jnp.where(grid.odd, other, carry), jnp.where(grid.odd, carry, other)], axis=0
    )


def adjoint_of(diag_factor, diag_cot, inverse):
    inner = lower_half(mm_t(diag_factor, jnp.tril(diag_cot)))
    return lower_half(mm(mm_t(inverse, inner), inverse))


def shards(saved_factor, cotangent):
    grid = Grid()
    row, col = grid.row, grid.col
    last, near = grid.col_count - 1, grid.col_count - 2
    planes = list(range(grid.col_count))
    solved_rows = range(NP, grid.row_count)
    below = row >= NP

    if grid.paired:
        mine = jnp.where(grid.odd, saved_factor[HALF:], saved_factor[:HALF])
        given = jnp.where(grid.odd, saved_factor[:HALF], saved_factor[HALF:])
        mate = grid.within(given, [(r, r ^ 1) for r in range(NP)], planes)
        seeds = [
            jnp.where(row == root, mine, jnp.where(row == root ^ 1, mate, 0.0)) for root in (2, 1, 0)
        ]
    else:
        seeds = [jnp.where(row == root, saved_factor, 0.0) for root in (2, 1, 0)]
    strip0_right = spread(grid, seeds[0][:, NB:], 2)
    strip0_left = spread(grid, seeds[0][:, :NB], 2)
    strip1_left = spread(grid, seeds[1][:, :NB], 1)
    strip1_right = spread(grid, seeds[1][:, NB:], 1)
    strip2 = spread(grid, seeds[2], 0)
    strip2_right = strip2[:, NB:]

    first_inverse = invert(strip0_right)
    second_diag = jnp.where(col == last, strip1_left, strip2_right)
    second_inverse = invert(second_diag)

    solved0 = mm(cotangent[:, NB:], first_inverse)
    solved1 = mm(cotangent[:, :NB] - mm(solved0, strip0_left), second_inverse)
    starts = {1: solved0, 2: solved1}

    steps = last + NP
    held = {}
    running = cotangent
    came = None
    state = {}
    for step in range(1, steps + 1):
        if step in starts:
            now = jnp.where(below & (col == last), starts[step], 0.0)
            if came is not None:
                now = now + came
        elif step == 4:
            solved2 = mm(
                cotangent[:, NB:] - mm(held[2], strip0_right) - mm(held[3], strip1_right),
                second_inverse,
            )
            now = jnp.where(below & (col == near), solved2, 0.0)
            if came is not None:
                now = now + came
        else:
            now = came
        held[step] = now
        which = {c: step - 1 - (last - c) for c in planes}
        roots = {
            c: 2 - k for c, k in which.items() if 0 <= k < NP and not (c == last and k == 2)
        }
        onward = [c for c in roots if c > 0]
        came = grid.down(now, solved_rows, onward) if onward else jnp.zeros_like(now)
        running = running - gather_sum(grid, mm_t(now, saved_factor), roots)
        if step == 1:
            adj0 = adjoint_of(strip0_right, running[:, NB:], first_inverse)
            sym0 = adj0 + adj0.T
            cross = mm(running[:, :NB] - mm(sym0, strip0_left), second_inverse)
            crossed = grid.send(cross, [((2, last), (1, last))])
        if step == 2:
            adj1 = adjoint_of(
                second_diag, running[:, :NB] - mm_t(crossed, strip0_left), second_inverse
            )
            sym1 = adj1 + adj1.T

    blocks = []
    for k in range(NP):
        block = held[k + 1]
        for hop in range(1, grid.col_count):
            if k + 1 + hop in held:
                block = jnp.where(col == last - hop, held[k + 1 + hop], block)
        blocks.append(block)

    hop0 = grid.send(sym0, [((2, last), (2, near))])
    hop1 = grid.send(cross, [((2, last), (2, near))])
    hop2 = grid.send(crossed, [((1, last), (1, near))])
    hop3 = grid.send(sym1, [((1, last), (1, near))])
    left0 = hop0 + hop2.T
    left1 = hop1 + hop3
    cross2 = mm(
        running[:, NB:] - mm(left0, strip0_right) - mm(left1, strip1_right), second_inverse
    )
    from2 = grid.send(cross2, [((2, near), (0, near))])
    from1 = grid.send(cross2, [((1, near), (0, near))])
    adj2 = adjoint_of(
        strip2_right,
        running[:, NB:] - mm_t(from2, strip0_right) - mm_t(from1, strip1_right),
        second_inverse,
    )
    sym2 = adj2 + adj2.T
    if near > 0:
        pair = jnp.stack([hop0 + hop2, hop1 + hop3])
        total = pair
        late = jnp.where(row == 0, from2, cross2)
        late_total = late
        square = sym2
        square_total = sym2
        for c in range(near, 0, -1):
            pair = grid.down(pair, (1, 2), [c])
            total = total + pair
            late = grid.down(late, (0, 1, 2), [c])
            late_total = jnp.where(col == near, late_total, 0.0) + late if c == near else late_total + late
            square = grid.down(square, (0,), [c])
            square_total = (
                jnp.where(col == near, square_total, 0.0) + square if c == near else square_total + square
            )
        mate = grid.within(late_total, [(1, 0)], range(near))
        other = jnp.where(col == near, from1, mate)
    else:
        total = jnp.stack([hop0 + hop2, hop1 + hop3])
        late_total = jnp.where(row == 0, from2, cross2)
        square_total = sym2
        other = from1
    blocks[0] = jnp.where(
        below, blocks[0], jnp.where(row == 2, total[0], jnp.where(row == 1, total[0], late_total).T)
    )
    blocks[1] = jnp.where(below, blocks[1], jnp.where(row == 0, other.T, total[1]))
    blocks[2] = jnp.where(below, blocks[2], jnp.where(row == 0, square_total, late_total))

    result = running
    strips = (
        jnp.concatenate([strip0_left, strip0_right], axis=1),
        jnp.concatenate([strip1_left, strip1_right], axis=1),
        strip2,
    )
    for block, strip in zip(blocks, strips):
        result = result - mm(block, strip)

    right = jnp.where(
        col == last,
        jnp.where(below, held[1], jnp.where(row == 2, adj0, cotangent[:, NB:])),
        jnp.where(
            col == near,
            jnp.where(row == 0, adj2, blocks[2]),
            result[:, NB:],
        ),
    )
    left = jnp.where(
        col == last,
        jnp.where(
            below,
            held[2],
            jnp.where(row == 2, cross, jnp.where(row == 1, adj1, cotangent[:, :NB])),
        ),
        result[:, :NB],
    )
    return jnp.concatenate([left, right], axis=1)


def solution(mesh):
    placed = (P("row", "col"), P("row", "col"))
    return jax.shard_map(
        shards, mesh=mesh, in_specs=placed, out_specs=P("row", "col"), check_vma=False
    )
```

time: 934 us -> 602 us (0.64)
  waiting for transfers between devices: 554 us -> 57 us
  starting transfers between devices: 1.3 us -> 256 us
  other arithmetic: 154 us -> 79.2 us
  matrix products: 121 us -> 72 us
  local copies, waits for them, and re-layouts: 79.5 us -> 113 us
  between operations: 14.8 us -> 2.4 us
  Pallas kernels: 0 us -> 11.3 us
    psum x7 -> x0, waiting for transfers between devices: 554 us -> none  [from_root(): return lax.psum(jnp.where(mine, shard, jnp.zeros_like(shard)), axis)]
    ppermute x0 -> x59, starting transfers between devices: none -> 256 us  [send(): return lax.ppermute(value, ('row', 'col'), flat)]
    another operation x9 -> x3, other arithmetic: 129 us -> 5.16 us  [shards(): pair = jnp.stack([hop0 + hop2, hop1 + hop3])]
    ppermute x0 -> x59, waiting for transfers between devices: none -> 57 us  [send(): return lax.ppermute(value, ('row', 'col'), flat)]
    another operation x41 -> x0, local copies, waits for them, and re-layouts: 40.7 us -> none  [the longest x40 37.9 us: shards(): lax.linalg.triangular_solve(diag_factor, identity, left_side=True, lower=...]
    add x0 -> x30, other arithmetic: none -> 37.3 us  [the longest x8 11.6 us: spread(): carry + grid.within(carry, [(a ^ base, b ^ base) for a, b in moves], planes)]
    dot_general x24 -> x32, matrix products: 97.8 us -> 72 us  [the longest x17 39 us: mm(): jnp.dot(left, right, precision=precision, preferred_element_type=jnp.floa...]
    another operation x21 -> x0, matrix products: 23.3 us -> none  [shards(): lax.linalg.triangular_solve(diag_factor, identity, left_side=True, lower=...]
  transfers between devices with their start and end apart: 7 -> 59, of which waited for: 7 -> 7; matrix products, arithmetic and copies ran while one was open for 15% -> 39% of each run, Pallas kernels for 0% -> 2%
where the time goes in v1:
time: 602 us; the launch traced here: 590 us
  starting transfers between devices  256 us (43%)
  local copies, waits for them, and re-layouts  113 us (19%)
  other arithmetic  79.2 us (13%)
  matrix products  72 us (12%)
  waiting for transfers between devices  57 us (9%)
  Pallas kernels  11.3 us (2%)
    ppermute x59, starting transfers between devices, send(): return lax.ppermute(value, ('row', 'col'), flat)  256 us
    ppermute x59, waiting for transfers between devices, send(): return lax.ppermute(value, ('row', 'col'), flat)  57 us
    dot_general x17, matrix products, mm(): jnp.dot(left, right, precision=precision, preferred_element_type=jnp.floa...  39 us
    gather x6, local copies, waits for them, and re-layouts, lower_half(): return jnp.tril(matrix) - 0.5 * jnp.diag(jnp.diag(matrix))  35.6 us
    dot_general x15, matrix products, mm_t(): lax.dot_general(left, right, (((0,), (0,)), ((), ())), precision=precisio...  32.9 us
    unnamed x189, local copies, waits for them, and re-layouts  20.7 us
    ppermute x6, local copies, waits for them, and re-layouts, send(): return lax.ppermute(value, ('row', 'col'), flat)  12.9 us
  transfers between devices with their start and end apart: 59, of which 7 were waited for; matrix products, arithmetic and copies ran while one was open for 39% of the time, Pallas kernels for 2%

profile of v1, /device:TPU:1, one launch (start us, length us, event | category | flops | bytes accessed | tf_op | source)
XLA Modules:
  0.0 590.1 jit_solution(2111260019379087274)
XLA Ops:
  3.6 8.3 %collective-permute-start = (f32[256,1024]{0,1:T(8,128)}, f32[256,1024]{0,1:T(8,128)S(1)}, u32[]{:S(2)}, u32[]{:S(2)}) collective-permute-start(f32[256,1024]{0,1:T(8,128)} %broadcast_select_fusion.6), channel_id=1, source_target_pairs={{0,4},{4,0},{8,12},{1,5},{5,1},{9,13},{2,6},{6,2},{10,14},{3,7},{7... | collective-permute-start | bytes 3145736 | tf_op jit(solution)/shard_map/ppermute | solution.py:104
  15.5 2.5 copy.92
  19.2 7.9 %collective-permute-start.1 = (f32[256,512]{0,1:T(8,128)}, f32[256,512]{0,1:T(8,128)}, u32[]{:S(2)}, u32[]{:S(2)}) collective-permute-start(f32[256,512]{0,1:T(8,128)} %get-tuple-element.46), channel_id=1, source_target_pairs={{8,24},{12,4},{9,25},{13,5},{10,26},{14,6},{11,27},{15,7}} | collective-permute-start | bytes 1572872 | tf_op jit(solution)/shard_map/ppermute | solution.py:104
  27.1 7.0 %collective-permute-start.4 = (f32[256,512]{0,1:T(8,128)}, f32[256,512]{0,1:T(8,128)}, u32[]{:S(2)}, u32[]{:S(2)}) collective-permute-start(f32[256,512]{0,1:T(8,128)} %get-tuple-element.45), channel_id=1, source_target_pairs={{8,24},{12,4},{9,25},{13,5},{10,26},{14,6},{11,27},{15,7}} | collective-permute-start | bytes 1572872 | tf_op jit(solution)/shard_map/ppermute | solution.py:104
  36.8 4.5 collective-permute-start.10
  41.3 4.8 collective-permute-start.28
  46.1 2.6 collective-permute-start.7
  50.9 5.3 collective-permute-start.2
  56.2 7.8 %collective-permute-start.5 = (f32[256,512]{0,1:T(8,128)}, f32[256,512]{0,1:T(8,128)}, u32[]{:S(2)}, u32[]{:S(2)}) collective-permute-start(f32[256,512]{0,1:T(8,128)} %get-tuple-element.43), channel_id=1, source_target_pairs={{24,16},{4,20},{12,28},{8,0},{25,17},{5,21},{13,29},{9,1},{26,18},... | collective-permute-start | bytes 1572872 | tf_op jit(solution)/shard_map/ppermute | solution.py:104
  65.2 2.6 collective-permute-start.8
  68.0 5.9 collective-permute-start.3
  73.9 3.0 copy.87
  79.0 5.2 collective-permute-start.6
  85.6 8.0 %collective-permute-start.11 = (f32[256,1024]{1,0:T(8,128)S(1)}, f32[256,1024]{1,0:T(8,128)}, u32[]{:S(2)}, u32[]{:S(2)}) collective-permute-start(f32[256,1024]{1,0:T(8,128)S(1)} %add.154), channel_id=1, source_target_pairs={{16,24},{12,28},{4,20},{0,8},{17,25},{13,29},{5,21},{1,9},{18,26},... | collective-permute-start | bytes 3145736 | tf_op jit(solution)/shard_map/ppermute | solution.py:104
  95.6 4.8 collective-permute-start.9
  102.0 5.6 invert.2
  113.1 4.5 collective-permute-start.29
  125.4 2.9 convolution_subtract_fusion.3
  133.9 5.6 invert.3
  141.6 2.5 copy.117
  144.1 15.3 %collective-permute-start.23 = (f32[512,512]{0,1:T(8,128)}, f32[512,512]{0,1:T(8,128)}, u32[]{:S(2)}, u32[]{:S(2)}) collective-permute-start(f32[512,512]{0,1:T(8,128)} %copy.117), channel_id=1, source_target_pairs={{14,13},{18,17},{22,21},{26,25},{30,29},{15,14},{19,18},{23,22},{2... | collective-permute-start | bytes 3145736 | tf_op jit(solution)/shard_map/ppermute | solution.py:104
  161.0 3.5 fusion.71
  164.7 7.6 %collective-permute-start.14 = (f32[256,1024]{0,1:T(8,128)S(1)}, f32[256,1024]{0,1:T(8,128)S(1)}, u32[]{:S(2)}, u32[]{:S(2)}) collective-permute-start(f32[256,1024]{0,1:T(8,128)S(1)} %slice_select_fusion.9), channel_id=1, source_target_pairs={{3,7},{7,3},{11,15},{15,11},{19,23},{23,19},{27,31},{31,27}} | collective-permute-start | bytes 3145736 | tf_op jit(solution)/shard_map/ppermute | solution.py:104
  175.2 19.3 %collective-permute-start.18 = (f32[256,1024]{0,1:T(8,128)S(1)}, f32[256,1024]{0,1:T(8,128)S(1)}, u32[]{:S(2)}, u32[]{:S(2)}) collective-permute-start(f32[256,1024]{0,1:T(8,128)S(1)} %slice_select_fusion.8), channel_id=1, source_target_pairs={{2,6},{6,2},{10,14},{14,10},{18,22},{22,18},{26,30},{30,26},{3,7},... | collective-permute-start | bytes 3145736 | tf_op jit(solution)/shard_map/ppermute | solution.py:104
  199.7 3.1 fusion.135
  202.9 20.5 %collective-permute-start.24 = (f32[256,1024]{0,1:T(8,128)S(1)}, f32[256,1024]{0,1:T(8,128)S(1)}, u32[]{:S(2)}, u32[]{:S(2)}) collective-permute-start(f32[256,1024]{0,1:T(8,128)S(1)} %slice_select_fusion.7), channel_id=1, source_target_pairs={{1,5},{5,1},{9,13},{13,9},{17,21},{21,17},{25,29},{29,25},{2,6},{6... | collective-permute-start | bytes 3145736 | tf_op jit(solution)/shard_map/ppermute | solution.py:104
  225.4 7.2 %collective-permute-start.32 = (f32[256,1024]{0,1:T(8,128)S(1)}, f32[256,1024]{0,1:T(8,128)S(1)}, u32[]{:S(2)}, u32[]{:S(2)}) collective-permute-start(f32[256,1024]{0,1:T(8,128)S(1)} %slice_select_fusion.6), channel_id=1, source_target_pairs={{0,4},{4,0},{8,12},{12,8},{16,20},{20,16},{24,28},{28,24},{1,5},{5... | collective-permute-start | bytes 3145736 | tf_op jit(solution)/shard_map/ppermute | solution.py:104
  234.6 10.4 %collective-permute-start.37 = (f32[256,1024]{0,1:T(8,128)S(1)}, f32[256,1024]{0,1:T(8,128)S(1)}, u32[]{:S(2)}, u32[]{:S(2)}) collective-permute-start(f32[256,1024]{0,1:T(8,128)S(1)} %slice_select_fusion.5), channel_id=1, source_target_pairs={{0,4},{4,0},{8,12},{12,8},{16,20},{20,16},{24,28},{28,24},{1,5},{5... | collective-permute-start | bytes 3145736 | tf_op jit(solution)/shard_map/ppermute | solution.py:104
  246.2 7.7 %collective-permute-start.19 = (f32[256,1024]{0,1:T(8,128)S(1)}, f32[256,1024]{0,1:T(8,128)S(1)}, u32[]{:S(2)}, u32[]{:S(2)}) collective-permute-start(f32[256,1024]{0,1:T(8,128)S(1)} %select_add_fusion.4), channel_id=1, source_target_pairs={{18,26},{22,6},{30,14},{2,10},{27,19},{31,15},{23,7},{11,3}} | collective-permute-start | bytes 3145736 | tf_op jit(solution)/shard_map/ppermute | solution.py:104
  254.1 7.1 %collective-permute-start.25 = (f32[256,1024]{0,1:T(8,128)S(1)}, f32[256,1024]{0,1:T(8,128)S(1)}, u32[]{:S(2)}, u32[]{:S(2)}) collective-permute-start(f32[256,1024]{0,1:T(8,128)S(1)} %select_add_fusion.3), channel_id=1, source_target_pairs={{17,25},{21,5},{29,13},{1,9},{26,18},{30,14},{22,6},{10,2}} | collective-permute-start | bytes 3145736 | tf_op jit(solution)/shard_map/ppermute | solution.py:104
  261.4 6.4 %collective-permute-start.33 = (f32[256,1024]{0,1:T(8,128)S(1)}, f32[256,1024]{0,1:T(8,128)S(1)}, u32[]{:S(2)}, u32[]{:S(2)}) collective-permute-start(f32[256,1024]{0,1:T(8,128)S(1)} %select_add_fusion.2), channel_id=1, source_target_pairs={{16,24},{20,4},{28,12},{0,8},{25,17},{29,13},{21,5},{9,1},{26,18},... | collective-permute-start | bytes 3145736 | tf_op jit(solution)/shard_map/ppermute | solution.py:104
  268.7 6.5 %collective-permute-start.38 = (f32[256,1024]{0,1:T(8,128)S(1)}, f32[256,1024]{0,1:T(8,128)S(1)}, u32[]{:S(2)}, u32[]{:S(2)}) collective-permute-start(f32[256,1024]{0,1:T(8,128)S(1)} %select_add_fusion.1), channel_id=1, source_target_pairs={{24,16},{28,12},{20,4},{8,0},{25,17},{29,13},{21,5},{9,1}} | collective-permute-start | bytes 3145736 | tf_op jit(solution)/shard_map/ppermute | solution.py:104
  277.1 5.1 collective-permute-done.33
  284.1 3.8 collective-permute-start.34
  319.7 14.0 %collective-permute-done.43 = f32[256,1024]{0,1:T(8,128)S(1)} collective-permute-done((f32[256,1024]{0,1:T(8,128)S(1)}, f32[256,1024]{0,1:T(8,128)S(1)}, u32[]{:S(2)}, u32[]{:S(2)}) %collective-permute-start.43) | collective-permute-done | bytes 1048608 | tf_op jit(solution)/shard_map/ppermute | solution.py:104
  343.9 2.5 copy.104
  346.5 8.7 %gather_fusion = f32[512]{0:T(512)S(1)} fusion(f32[512,512]{1,0:T(8,128)} %fusion.37, s32[512]{0:T(512)S(1)} %bitcast.95), kind=kCustom, calls=%fused_computation | custom fusion | bytes 8192 | tf_op jit(solution)/shard_map/jit(_diag)/jit(diagonal)/cond/branch_0_fun/gather | solution.py:31
  355.2 3.1 fusion.65
  360.3 2.6 copy.105
  362.9 8.7 %gather_fusion.1 = f32[512]{0:T(512)S(1)} fusion(f32[512,512]{0,1:T(8,128)} %fusion.133, s32[512]{0:T(512)S(1)} %bitcast.96), kind=kCustom, calls=%fused_computation.1 | custom fusion | bytes 8192 | tf_op jit(solution)/shard_map/jit(_diag)/jit(diagonal)/cond/branch_0_fun/gather | solution.py:31
  371.7 3.4 fusion.47
  381.5 2.7 add.178
  384.1 6.4 %collective-permute-start.45 = (f32[256,1024]{0,1:T(8,128)}, f32[256,1024]{0,1:T(8,128)}, u32[]{:S(2)}, u32[]{:S(2)}) collective-permute-start(f32[256,1024]{0,1:T(8,128)} %add.178), channel_id=1, source_target_pairs={{4,0}} | collective-permute-start | bytes 3145736 | tf_op jit(solution)/shard_map/ppermute | solution.py:104
  393.8 4.5 gather_fusion.2
  403.6 4.5 gather_fusion.3
  415.1 2.9 subtract_add_fusion
  421.4 2.6 copy.129
  435.3 2.5 copy.133
  442.6 2.7 fusion.77
  445.4 2.6 fusion.23
  466.8 2.9 fusion.109
  469.7 2.7 copy.158
  472.4 4.5 gather_fusion.4
  476.9 3.1 fusion.48
  481.4 4.5 gather_fusion.5
  495.4 2.6 copy.136
  498.0 2.6 copy.138
  505.8 31.1 %collective-permute-done.54 = f32[512,512]{0,1:T(8,128)} collective-permute-done((f32[512,512]{0,1:T(8,128)}, f32[512,512]{0,1:T(8,128)}, u32[]{:S(2)}, u32[]{:S(2)}) %collective-permute-start.54) | collective-permute-done | bytes 1048608 | tf_op jit(solution)/shard_map/ppermute | solution.py:104
  536.9 6.1 %fusion.75 = (f32[512,512]{0,1:T(8,128)}, f32[512,512]{0,1:T(8,128)}, f32[512,512]{0,1:T(8,128)}) fusion(f32[512,512]{0,1:T(8,128)} %copy-done.48, f32[512]{0:T(512)S(1)} %gather_fusion.5, pred[]{:T(512)S(6)} %eq.53, f32[512,512]{0,1:T(8,128)} %collective-permute-done.58, f32[512,512]{0,1:T(8,128)} %collective-permute-done.57, f32[512,512]{0,1:T(8,128)} %copy-done.83, ...), kind=kLoop, calls=%fused_computation.142 | loop fusion | flops 4718592 | bytes 14682117 | tf_op jit(solution)/shard_map/jit(_where)/select_n | solution.py:312
  543.0 18.9 %collective-permute-start.56 = (f32[512,512]{0,1:T(8,128)}, f32[512,512]{0,1:T(8,128)}, u32[]{:S(2)}, u32[]{:S(2)}) collective-permute-start(f32[512,512]{0,1:T(8,128)} %get-tuple-element.7), channel_id=1, source_target_pairs={{4,0},{5,1}} | collective-permute-start | bytes 3145736 | tf_op jit(solution)/shard_map/ppermute | solution.py:104
  564.5 4.6 fusion
  569.1 3.0 add_add_fusion
  577.2 4.5 fusion.6
  582.7 4.3 subtract_subtract_fusion
  (382 shorter events, 193.1 us)
Async XLA Ops:
  3.6 10.7 %collective-permute-start = (f32[256,1024]{0,1:T(8,128)}, f32[256,1024]{0,1:T(8,128)S(1)}, u32[]{:S(2)}, u32[]{:S(2)}) collective-permute-start(f32[256,1024]{0,1:T(8,128)} %broadcast_select_fusion.6), channel_id=1, source_target_pairs={{0,4},{4,0},{8,12},{1,5},{5,1},{9,13},{2,6},{6,2},{10,14},{3,7},{7... | collective-permute-start | bytes 3145736 | tf_op jit(solution)/shard_map/ppermute | solution.py:104
  19.2 29.5 %collective-permute-start.1 = (f32[256,512]{0,1:T(8,128)}, f32[256,512]{0,1:T(8,128)}, u32[]{:S(2)}, u32[]{:S(2)}) collective-permute-start(f32[256,512]{0,1:T(8,128)} %get-tuple-element.46), channel_id=1, source_target_pairs={{8,24},{12,4},{9,25},{13,5},{10,26},{14,6},{11,27},{15,7}} | collective-permute-start | bytes 1572872 | tf_op jit(solution)/shard_map/ppermute | solution.py:104
  27.1 21.7 %collective-permute-start.4 = (f32[256,512]{0,1:T(8,128)}, f32[256,512]{0,1:T(8,128)}, u32[]{:S(2)}, u32[]{:S(2)}) collective-permute-start(f32[256,512]{0,1:T(8,128)} %get-tuple-element.45), channel_id=1, source_target_pairs={{8,24},{12,4},{9,25},{13,5},{10,26},{14,6},{11,27},{15,7}} | collective-permute-start | bytes 1572872 | tf_op jit(solution)/shard_map/ppermute | solution.py:104
  36.8 47.4 %collective-permute-start.10 = (f32[256,1024]{1,0:T(8,128)S(1)}, f32[256,1024]{1,0:T(8,128)}, u32[]{:S(2)}, u32[]{:S(2)}) collective-permute-start(f32[256,1024]{1,0:T(8,128)S(1)} %select_select_fusion.2), channel_id=1, source_target_pairs={{0,16},{4,12},{1,17},{5,13},{2,18},{6,14},{3,19},{7,15}} | collective-permute-start | bytes 3145736 | tf_op jit(solution)/shard_map/ppermute | solution.py:104
  41.3 22.7 %collective-permute-start.28 = (f32[256,512]{0,1:T(8,128)S(1)}, f32[256,512]{0,1:T(8,128)S(1)}, u32[]{:S(2)}, u32[]{:S(2)}) collective-permute-start(f32[256,512]{0,1:T(8,128)S(1)} %get-tuple-element.37), channel_id=1, source_target_pairs={{0,16},{4,12},{1,17},{5,13},{2,18},{6,14},{3,19},{7,15}} | collective-permute-start | bytes 1572872 | tf_op jit(solution)/shard_map/ppermute | solution.py:104
  46.1 17.9 %collective-permute-start.7 = (f32[256,512]{0,1:T(8,128)S(1)}, f32[256,512]{0,1:T(8,128)S(1)}, u32[]{:S(2)}, u32[]{:S(2)}) collective-permute-start(f32[256,512]{0,1:T(8,128)S(1)} %get-tuple-element.38), channel_id=1, source_target_pairs={{0,16},{4,12},{1,17},{5,13},{2,18},{6,14},{3,19},{7,15}} | collective-permute-start | bytes 1572872 | tf_op jit(solution)/shard_map/ppermute | solution.py:104
  50.9 17.0 %collective-permute-start.2 = (f32[256,512]{0,1:T(8,128)S(1)}, f32[256,512]{0,1:T(8,128)S(1)}, u32[]{:S(2)}, u32[]{:S(2)}) collective-permute-start(f32[256,512]{0,1:T(8,128)S(1)} %get-tuple-element.44), channel_id=1, source_target_pairs={{24,16},{4,20},{12,28},{8,0},{25,17},{5,21},{13,29},{9,1},{26,18},... | collective-permute-start | bytes 1572872 | tf_op jit(solution)/shard_map/ppermute | solution.py:104
  56.2 20.7 %collective-permute-start.5 = (f32[256,512]{0,1:T(8,128)}, f32[256,512]{0,1:T(8,128)}, u32[]{:S(2)}, u32[]{:S(2)}) collective-permute-start(f32[256,512]{0,1:T(8,128)} %get-tuple-element.43), channel_id=1, source_target_pairs={{24,16},{4,20},{12,28},{8,0},{25,17},{5,21},{13,29},{9,1},{26,18},... | collective-permute-start | bytes 1572872 | tf_op jit(solution)/shard_map/ppermute | solution.py:104
  65.2 28.4 %collective-permute-start.8 = (f32[256,512]{0,1:T(8,128)}, f32[256,512]{0,1:T(8,128)}, u32[]{:S(2)}, u32[]{:S(2)}) collective-permute-start(f32[256,512]{0,1:T(8,128)} %get-tuple-element.36), channel_id=1, source_target_pairs={{16,24},{12,28},{4,20},{0,8},{17,25},{13,29},{5,21},{1,9},{18,26},... | collective-permute-start | bytes 1572872 | tf_op jit(solution)/shard_map/ppermute | solution.py:104
  68.0 32.4 %collective-permute-start.3 = (f32[256,512]{0,1:T(8,128)S(1)}, f32[256,512]{0,1:T(8,128)S(1)}, u32[]{:S(2)}, u32[]{:S(2)}) collective-permute-start(f32[256,512]{0,1:T(8,128)S(1)} %add.149), channel_id=1, source_target_pairs={{0,4},{4,0},{8,12},{12,8},{16,20},{20,16},{24,28},{28,24},{1,5},{5... | collective-permute-start | bytes 1572872 | tf_op jit(solution)/shard_map/ppermute | solution.py:104
  79.0 44.5 %collective-permute-start.6 = (f32[256,512]{0,1:T(8,128)}, f32[256,512]{0,1:T(8,128)}, u32[]{:S(2)}, u32[]{:S(2)}) collective-permute-start(f32[256,512]{0,1:T(8,128)} %add.151), channel_id=1, source_target_pairs={{0,4},{4,0},{8,12},{12,8},{16,20},{20,16},{24,28},{28,24},{1,5},{5... | collective-permute-start | bytes 1572872 | tf_op jit(solution)/shard_map/ppermute | solution.py:104
  85.6 25.9 %collective-permute-start.11 = (f32[256,1024]{1,0:T(8,128)S(1)}, f32[256,1024]{1,0:T(8,128)}, u32[]{:S(2)}, u32[]{:S(2)}) collective-permute-start(f32[256,1024]{1,0:T(8,128)S(1)} %add.154), channel_id=1, source_target_pairs={{16,24},{12,28},{4,20},{0,8},{17,25},{13,29},{5,21},{1,9},{18,26},... | collective-permute-start | bytes 3145736 | tf_op jit(solution)/shard_map/ppermute | solution.py:104
  95.6 21.9 %collective-permute-start.9 = (f32[256,512]{0,1:T(8,128)}, f32[256,512]{0,1:T(8,128)}, u32[]{:S(2)}, u32[]{:S(2)}) collective-permute-start(f32[256,512]{0,1:T(8,128)} %add.153), channel_id=1, source_target_pairs={{0,4},{4,0},{8,12},{12,8},{16,20},{20,16},{24,28},{28,24},{1,5},{5... | collective-permute-start | bytes 1572872 | tf_op jit(solution)/shard_map/ppermute | solution.py:104
  109.8 18.4 %collective-permute-start.13 = (f32[512,512]{0,1:T(8,128)}, f32[512,512]{0,1:T(8,128)}, u32[]{:S(2)}, u32[]{:S(2)}) collective-permute-start(f32[512,512]{0,1:T(8,128)} %select_bitcast_fusion), channel_id=1, source_target_pairs={{15,14},{19,18},{23,22},{27,26},{31,30}} | collective-permute-start | bytes 3145736 | tf_op jit(solution)/shard_map/ppermute | solution.py:104
  112.8 18.0 %collective-permute-start.12 = (f32[256,1024]{1,0:T(8,128)S(1)}, f32[256,1024]{1,0:T(8,128)}, u32[]{:S(2)}, u32[]{:S(2)}) collective-permute-start(f32[256,1024]{1,0:T(8,128)S(1)} %add.155), channel_id=1, source_target_pairs={{0,4},{4,0},{8,12},{12,8},{16,20},{20,16},{24,28},{28,24},{1,5},{5... | collective-permute-start | bytes 3145736 | tf_op jit(solution)/shard_map/ppermute | solution.py:104
  113.1 46.4 %collective-permute-start.29 = (f32[256,512]{0,1:T(8,128)}, f32[256,512]{0,1:T(8,128)}, u32[]{:S(2)}, u32[]{:S(2)}) collective-permute-start(f32[256,512]{0,1:T(8,128)} %get-tuple-element.35), channel_id=1, source_target_pairs={{16,24},{12,28},{4,20},{0,8},{17,25},{13,29},{5,21},{1,9},{18,26},... | collective-permute-start | bytes 1572872 | tf_op jit(solution)/shard_map/ppermute | solution.py:104
  144.1 28.3 %collective-permute-start.23 = (f32[512,512]{0,1:T(8,128)}, f32[512,512]{0,1:T(8,128)}, u32[]{:S(2)}, u32[]{:S(2)}) collective-permute-start(f32[512,512]{0,1:T(8,128)} %copy.117), channel_id=1, source_target_pairs={{14,13},{18,17},{22,21},{26,25},{30,29},{15,14},{19,18},{23,22},{2... | collective-permute-start | bytes 3145736 | tf_op jit(solution)/shard_map/ppermute | solution.py:104
  160.8 11.5 %collective-permute-start.30 = (f32[256,512]{0,1:T(8,128)S(1)}, f32[256,512]{0,1:T(8,128)S(1)}, u32[]{:S(2)}, u32[]{:S(2)}) collective-permute-start(f32[256,512]{0,1:T(8,128)S(1)} %add.168), channel_id=1, source_target_pairs={{0,4},{4,0},{8,12},{12,8},{16,20},{20,16},{24,28},{28,24},{1,5},{5... | collective-permute-start | bytes 1572872 | tf_op jit(solution)/shard_map/ppermute | solution.py:104
  164.7 80.4 %collective-permute-start.14 = (f32[256,1024]{0,1:T(8,128)S(1)}, f32[256,1024]{0,1:T(8,128)S(1)}, u32[]{:S(2)}, u32[]{:S(2)}) collective-permute-start(f32[256,1024]{0,1:T(8,128)S(1)} %slice_select_fusion.9), channel_id=1, source_target_pairs={{3,7},{7,3},{11,15},{15,11},{19,23},{23,19},{27,31},{31,27}} | collective-permute-start | bytes 3145736 | tf_op jit(solution)/shard_map/ppermute | solution.py:104
  172.4 22.2 %copy-start.38 = (f32[256,512]{0,1:T(8,128)}, f32[256,512]{0,1:T(8,128)S(1)}, u32[]{:S(2)}) copy-start(f32[256,512]{0,1:T(8,128)S(1)} %get-tuple-element.33) | copy-start | bytes 1572868
  172.4 22.2 %copy-start.41 = (f32[256,512]{0,1:T(8,128)}, f32[256,512]{0,1:T(8,128)S(1)}, u32[]{:S(2)}) copy-start(f32[256,512]{0,1:T(8,128)S(1)} %get-tuple-element.34) | copy-start | bytes 1572868
  172.4 25.5 %collective-permute-start.31 = (f32[512,512]{0,1:T(8,128)}, f32[512,512]{0,1:T(8,128)S(1)}, u32[]{:S(2)}, u32[]{:S(2)}) collective-permute-start(f32[512,512]{0,1:T(8,128)} %collective-permute-done.23), channel_id=1, source_target_pairs={{13,12},{17,16},{21,20},{25,24},{29,28},{14,13},{18,17},{22,21},{2... | collective-permute-start | bytes 3145736 | tf_op jit(solution)/shard_map/ppermute | solution.py:104
  175.1 21.6 %copy-start.7 = (f32[512,1024]{0,1:T(8,128)S(1)}, f32[512,1024]{0,1:T(8,128)}, u32[]{:S(2)}) copy-start(f32[512,1024]{0,1:T(8,128)} %copy.87) | copy-start | bytes 6291460
  175.2 70.8 %collective-permute-start.18 = (f32[256,1024]{0,1:T(8,128)S(1)}, f32[256,1024]{0,1:T(8,128)S(1)}, u32[]{:S(2)}, u32[]{:S(2)}) collective-permute-start(f32[256,1024]{0,1:T(8,128)S(1)} %slice_select_fusion.8), channel_id=1, source_target_pairs={{2,6},{6,2},{10,14},{14,10},{18,22},{22,18},{26,30},{30,26},{3,7},... | collective-permute-start | bytes 3145736 | tf_op jit(solution)/shard_map/ppermute | solution.py:104
  198.9 24.5 %copy-start.19 = (f32[512,512]{0,1:T(8,128)}, f32[512,512]{0,1:T(8,128)S(1)}, u32[]{:S(2)}) copy-start(f32[512,512]{0,1:T(8,128)S(1)} %fusion.94) | copy-start | bytes 3145732
  198.9 33.7 %collective-permute-start.36 = (f32[512,512]{0,1:T(8,128)S(1)}, f32[512,512]{0,1:T(8,128)S(1)}, u32[]{:S(2)}, u32[]{:S(2)}) collective-permute-start(f32[512,512]{0,1:T(8,128)S(1)} %fusion.94), channel_id=1, source_target_pairs={{13,12},{17,16},{21,20},{25,24},{29,28},{14,13},{18,17},{22,21},{2... | collective-permute-start | bytes 3145736 | tf_op jit(solution)/shard_map/ppermute | solution.py:104
  202.9 51.0 %collective-permute-start.24 = (f32[256,1024]{0,1:T(8,128)S(1)}, f32[256,1024]{0,1:T(8,128)S(1)}, u32[]{:S(2)}, u32[]{:S(2)}) collective-permute-start(f32[256,1024]{0,1:T(8,128)S(1)} %slice_select_fusion.7), channel_id=1, source_target_pairs={{1,5},{5,1},{9,13},{13,9},{17,21},{21,17},{25,29},{29,25},{2,6},{6... | collective-permute-start | bytes 3145736 | tf_op jit(solution)/shard_map/ppermute | solution.py:104
  225.4 35.7 %collective-permute-start.32 = (f32[256,1024]{0,1:T(8,128)S(1)}, f32[256,1024]{0,1:T(8,128)S(1)}, u32[]{:S(2)}, u32[]{:S(2)}) collective-permute-start(f32[256,1024]{0,1:T(8,128)S(1)} %slice_select_fusion.6), channel_id=1, source_target_pairs={{0,4},{4,0},{8,12},{12,8},{16,20},{20,16},{24,28},{28,24},{1,5},{5... | collective-permute-start | bytes 3145736 | tf_op jit(solution)/shard_map/ppermute | solution.py:104
  232.6 35.1 %copy-start.44 = (f32[512,512]{0,1:T(8,128)}, f32[512,512]{0,1:T(8,128)S(1)}, u32[]{:S(2)}) copy-start(f32[512,512]{0,1:T(8,128)S(1)} %collective-permute-done.36) | copy-start | bytes 3145732
  234.6 33.1 %collective-permute-start.37 = (f32[256,1024]{0,1:T(8,128)S(1)}, f32[256,1024]{0,1:T(8,128)S(1)}, u32[]{:S(2)}, u32[]{:S(2)}) collective-permute-start(f32[256,1024]{0,1:T(8,128)S(1)} %slice_select_fusion.5), channel_id=1, source_target_pairs={{0,4},{4,0},{8,12},{12,8},{16,20},{20,16},{24,28},{28,24},{1,5},{5... | collective-permute-start | bytes 3145736 | tf_op jit(solution)/shard_map/ppermute | solution.py:104
  245.2 23.5 %collective-permute-start.15 = (f32[256,1024]{0,1:T(8,128)S(1)}, f32[256,1024]{0,1:T(8,128)S(1)}, u32[]{:S(2)}, u32[]{:S(2)}) collective-permute-start(f32[256,1024]{0,1:T(8,128)S(1)} %select_add_fusion.5), channel_id=1, source_target_pairs={{19,27},{23,7},{31,15},{3,11}} | collective-permute-start | bytes 3145736 | tf_op jit(solution)/shard_map/ppermute | solution.py:104
  246.2 29.1 %collective-permute-start.19 = (f32[256,1024]{0,1:T(8,128)S(1)}, f32[256,1024]{0,1:T(8,128)S(1)}, u32[]{:S(2)}, u32[]{:S(2)}) collective-permute-start(f32[256,1024]{0,1:T(8,128)S(1)} %select_add_fusion.4), channel_id=1, source_target_pairs={{18,26},{22,6},{30,14},{2,10},{27,19},{31,15},{23,7},{11,3}} | collective-permute-start | bytes 3145736 | tf_op jit(solution)/shard_map/ppermute | solution.py:104
  254.1 22.1 %collective-permute-start.25 = (f32[256,1024]{0,1:T(8,128)S(1)}, f32[256,1024]{0,1:T(8,128)S(1)}, u32[]{:S(2)}, u32[]{:S(2)}) collective-permute-start(f32[256,1024]{0,1:T(8,128)S(1)} %select_add_fusion.3), channel_id=1, source_target_pairs={{17,25},{21,5},{29,13},{1,9},{26,18},{30,14},{22,6},{10,2}} | collective-permute-start | bytes 3145736 | tf_op jit(solution)/shard_map/ppermute | solution.py:104
  261.4 20.9 %collective-permute-start.33 = (f32[256,1024]{0,1:T(8,128)S(1)}, f32[256,1024]{0,1:T(8,128)S(1)}, u32[]{:S(2)}, u32[]{:S(2)}) collective-permute-start(f32[256,1024]{0,1:T(8,128)S(1)} %select_add_fusion.2), channel_id=1, source_target_pairs={{16,24},{20,4},{28,12},{0,8},{25,17},{29,13},{21,5},{9,1},{26,18},... | collective-permute-start | bytes 3145736 | tf_op jit(solution)/shard_map/ppermute | solution.py:104
  267.8 16.3 %collective-permute-start.41 = (f32[512,512]{0,1:T(8,128)S(1)}, f32[512,512]{0,1:T(8,128)S(1)}, u32[]{:S(2)}, u32[]{:S(2)}) collective-permute-start(f32[512,512]{0,1:T(8,128)S(1)} %collective-permute-done.36), channel_id=1, source_target_pairs={{13,12},{17,16},{21,20},{25,24},{29,28}} | collective-permute-start | bytes 3145736 | tf_op jit(solution)/shard_map/ppermute | solution.py:104
  268.7 24.5 %collective-permute-start.38 = (f32[256,1024]{0,1:T(8,128)S(1)}, f32[256,1024]{0,1:T(8,128)S(1)}, u32[]{:S(2)}, u32[]{:S(2)}) collective-permute-start(f32[256,1024]{0,1:T(8,128)S(1)} %select_add_fusion.1), channel_id=1, source_target_pairs={{24,16},{28,12},{20,4},{8,0},{25,17},{29,13},{21,5},{9,1}} | collective-permute-start | bytes 3145736 | tf_op jit(solution)/shard_map/ppermute | solution.py:104
  275.3 21.0 %collective-permute-start.16 = (f32[256,1024]{0,1:T(8,128)S(1)}, f32[256,1024]{0,1:T(8,128)S(1)}, u32[]{:S(2)}, u32[]{:S(2)}) collective-permute-start(f32[256,1024]{0,1:T(8,128)S(1)} %add.158), channel_id=1, source_target_pairs={{27,11},{7,15}} | collective-permute-start | bytes 3145736 | tf_op jit(solution)/shard_map/ppermute | solution.py:104
  276.2 22.5 %collective-permute-start.20 = (f32[256,1024]{0,1:T(8,128)S(1)}, f32[256,1024]{0,1:T(8,128)S(1)}, u32[]{:S(2)}, u32[]{:S(2)}) collective-permute-start(f32[256,1024]{0,1:T(8,128)S(1)} %add.162), channel_id=1, source_target_pairs={{26,10},{6,14},{19,3},{15,7}} | collective-permute-start | bytes 3145736 | tf_op jit(solution)/shard_map/ppermute | solution.py:104
  282.2 19.2 %collective-permute-start.26 = (f32[256,1024]{0,1:T(8,128)S(1)}, f32[256,1024]{0,1:T(8,128)S(1)}, u32[]{:S(2)}, u32[]{:S(2)}) collective-permute-start(f32[256,1024]{0,1:T(8,128)S(1)} %add.165), channel_id=1, source_target_pairs={{25,9},{5,13},{18,2},{14,6}} | collective-permute-start | bytes 3145736 | tf_op jit(solution)/shard_map/ppermute | solution.py:104
  284.1 21.7 %collective-permute-start.34 = (f32[256,1024]{0,1:T(8,128)}, f32[256,1024]{0,1:T(8,128)}, u32[]{:S(2)}, u32[]{:S(2)}) collective-permute-start(f32[256,1024]{0,1:T(8,128)} %add.171), channel_id=1, source_target_pairs={{24,8},{4,12},{17,1},{13,5},{18,2},{14,6}} | collective-permute-start | bytes 3145736 | tf_op jit(solution)/shard_map/ppermute | solution.py:104
  293.2 15.2 %collective-permute-start.42 = (f32[256,1024]{0,1:T(8,128)}, f32[256,1024]{0,1:T(8,128)}, u32[]{:S(2)}, u32[]{:S(2)}) collective-permute-start(f32[256,1024]{0,1:T(8,128)} %slice_select_fusion.4), channel_id=1, source_target_pairs={{0,4},{4,0},{8,12},{12,8},{16,20},{20,16},{24,28},{28,24}} | collective-permute-start | bytes 3145736 | tf_op jit(solution)/shard_map/ppermute | solution.py:104
  296.3 16.1 %collective-permute-start.39 = (f32[256,1024]{0,1:T(8,128)}, f32[256,1024]{0,1:T(8,128)}, u32[]{:S(2)}, u32[]{:S(2)}) collective-permute-start(f32[256,1024]{0,1:T(8,128)} %add.174), channel_id=1, source_target_pairs={{16,0},{12,4},{17,1},{13,5}} | collective-permute-start | bytes 3145736 | tf_op jit(solution)/shard_map/ppermute | solution.py:104
  298.7 16.7 %collective-permute-start.17 = (f32[256,1024]{0,1:T(8,128)}, f32[256,1024]{0,1:T(8,128)}, u32[]{:S(2)}, u32[]{:S(2)}) collective-permute-start(f32[256,1024]{0,1:T(8,128)} %add.159), channel_id=1, source_target_pairs={{15,11}} | collective-permute-start | bytes 3145736 | tf_op jit(solution)/shard_map/ppermute | solution.py:104
  302.5 15.6 %collective-permute-start.21 = (f32[256,1024]{0,1:T(8,128)}, f32[256,1024]{0,1:T(8,128)}, u32[]{:S(2)}, u32[]{:S(2)}) collective-permute-start(f32[256,1024]{0,1:T(8,128)} %add.163), channel_id=1, source_target_pairs={{14,10},{3,7}} | collective-permute-start | bytes 3145736 | tf_op jit(solution)/shard_map/ppermute | solution.py:104
  305.8 13.7 %collective-permute-start.27 = (f32[256,1024]{0,1:T(8,128)S(1)}, f32[256,1024]{0,1:T(8,128)S(1)}, u32[]{:S(2)}, u32[]{:S(2)}) collective-permute-start(f32[256,1024]{0,1:T(8,128)S(1)} %add.166), channel_id=1, source_target_pairs={{13,9},{2,6}} | collective-permute-start | bytes 3145736 | tf_op jit(solution)/shard_map/ppermute | solution.py:104
  308.4 27.9 %collective-permute-start.35 = (f32[256,1024]{0,1:T(8,128)S(1)}, f32[256,1024]{0,1:T(8,128)S(1)}, u32[]{:S(2)}, u32[]{:S(2)}) collective-permute-start(f32[256,1024]{0,1:T(8,128)S(1)} %add.172), channel_id=1, source_target_pairs={{12,8},{1,5},{6,2}} | collective-permute-start | bytes 3145736 | tf_op jit(solution)/shard_map/ppermute | solution.py:104
  312.4 21.2 %collective-permute-start.43 = (f32[256,1024]{0,1:T(8,128)S(1)}, f32[256,1024]{0,1:T(8,128)S(1)}, u32[]{:S(2)}, u32[]{:S(2)}) collective-permute-start(f32[256,1024]{0,1:T(8,128)S(1)} %select_add_fusion), channel_id=1, source_target_pairs={{24,16},{28,12},{20,4},{8,0}} | collective-permute-start | bytes 3145736 | tf_op jit(solution)/shard_map/ppermute | solution.py:104
  315.4 21.0 %collective-permute-start.40 = (f32[256,1024]{0,1:T(8,128)S(1)}, f32[256,1024]{0,1:T(8,128)S(1)}, u32[]{:S(2)}, u32[]{:S(2)}) collective-permute-start(f32[256,1024]{0,1:T(8,128)S(1)} %add.175), channel_id=1, source_target_pairs={{0,4},{5,1}} | collective-permute-start | bytes 3145736 | tf_op jit(solution)/shard_map/ppermute | solution.py:104
  334.8 46.7 %collective-permute-start.44 = (f32[256,1024]{0,1:T(8,128)}, f32[256,1024]{0,1:T(8,128)}, u32[]{:S(2)}, u32[]{:S(2)}) collective-permute-start(f32[256,1024]{0,1:T(8,128)} %add.177), channel_id=1, source_target_pairs={{16,0},{12,4}} | collective-permute-start | bytes 3145736 | tf_op jit(solution)/shard_map/ppermute | solution.py:104
  379.1 11.4 %collective-permute-start.22 = (f32[512,512]{1,0:T(8,128)}, f32[512,512]{1,0:T(8,128)S(1)}, u32[]{:S(2)}, u32[]{:S(2)}) collective-permute-start(f32[512,512]{1,0:T(8,128)} %fusion.38), channel_id=1, source_target_pairs={{11,7}} | collective-permute-start | bytes 3145736 | tf_op jit(solution)/shard_map/ppermute | solution.py:104
  379.8 62.7 %collective-permute-start.48 = (f32[512,512]{1,0:T(8,128)}, f32[512,512]{1,0:T(8,128)}, u32[]{:S(2)}, u32[]{:S(2)}) collective-permute-start(f32[512,512]{1,0:T(8,128)} %fusion.38), channel_id=1, source_target_pairs={{11,10}} | collective-permute-start | bytes 3145736 | tf_op jit(solution)/shard_map/ppermute | solution.py:104
  384.1 43.6 %collective-permute-start.45 = (f32[256,1024]{0,1:T(8,128)}, f32[256,1024]{0,1:T(8,128)}, u32[]{:S(2)}, u32[]{:S(2)}) collective-permute-start(f32[256,1024]{0,1:T(8,128)} %add.178), channel_id=1, source_target_pairs={{4,0}} | collective-permute-start | bytes 3145736 | tf_op jit(solution)/shard_map/ppermute | solution.py:104
  418.0 24.6 %collective-permute-start.49 = (f32[512,512]{1,0:T(8,128)}, f32[512,512]{1,0:T(8,128)}, u32[]{:S(2)}, u32[]{:S(2)}) collective-permute-start(f32[512,512]{1,0:T(8,128)} %subtract_add_fusion), channel_id=1, source_target_pairs={{7,6}} | collective-permute-start | bytes 3145736 | tf_op jit(solution)/shard_map/ppermute | solution.py:104
  419.6 25.7 %collective-permute-start.46 = (f32[512,512]{0,1:T(8,128)}, f32[512,512]{0,1:T(8,128)}, u32[]{:S(2)}, u32[]{:S(2)}) collective-permute-start(f32[512,512]{0,1:T(8,128)} %copy-done.73), channel_id=1, source_target_pairs={{11,10}} | collective-permute-start | bytes 3145736 | tf_op jit(solution)/shard_map/ppermute | solution.py:104
  425.9 19.5 %collective-permute-start.47 = (f32[512,512]{1,0:T(8,128)}, f32[512,512]{1,0:T(8,128)}, u32[]{:S(2)}, u32[]{:S(2)}) collective-permute-start(f32[512,512]{1,0:T(8,128)} %copy-done.90), channel_id=1, source_target_pairs={{7,6}} | collective-permute-start | bytes 3145736 | tf_op jit(solution)/shard_map/ppermute | solution.py:104
  450.0 12.6 %collective-permute-start.55 = (f32[512,512]{0,1:T(8,128)}, f32[512,512]{0,1:T(8,128)}, u32[]{:S(2)}, u32[]{:S(2)}) collective-permute-start(f32[512,512]{0,1:T(8,128)} %fusion.139), channel_id=1, source_target_pairs={{6,2}} | collective-permute-start | bytes 3145736 | tf_op jit(solution)/shard_map/ppermute | solution.py:104
  454.2 10.7 %collective-permute-start.52 = (f32[512,512]{0,1:T(8,128)}, f32[512,512]{0,1:T(8,128)S(1)}, u32[]{:S(2)}, u32[]{:S(2)}) collective-permute-start(f32[512,512]{0,1:T(8,128)} %fusion.139), channel_id=1, source_target_pairs={{10,2}} | collective-permute-start | bytes 3145736 | tf_op jit(solution)/shard_map/ppermute | solution.py:104
  460.3 30.8 %collective-permute-start.50 = (f32[2,512,512]{2,1,0:T(8,128)}, f32[2,512,512]{2,1,0:T(8,128)}, u32[]{:S(2)}, u32[]{:S(2)}) collective-permute-start(f32[2,512,512]{2,1,0:T(8,128)} %pad_maximum_fusion), channel_id=1, source_target_pairs={{6,5},{10,9}} | collective-permute-start | bytes 6291464 | tf_op jit(solution)/shard_map/ppermute | solution.py:104
  487.4 5.0 collective-permute-start.53
  489.3 4.4 collective-permute-start.57
  491.1 78.0 %collective-permute-start.51 = (f32[2,512,512]{2,1,0:T(8,128)}, f32[2,512,512]{2,1,0:T(8,128)}, u32[]{:S(2)}, u32[]{:S(2)}) collective-permute-start(f32[2,512,512]{2,1,0:T(8,128)} %collective-permute-done.50), channel_id=1, source_target_pairs={{5,4},{9,8}} | collective-permute-start | bytes 6291464 | tf_op jit(solution)/shard_map/ppermute | solution.py:104
  492.4 44.5 %collective-permute-start.54 = (f32[512,512]{0,1:T(8,128)}, f32[512,512]{0,1:T(8,128)}, u32[]{:S(2)}, u32[]{:S(2)}) collective-permute-start(f32[512,512]{0,1:T(8,128)} %collective-permute-done.53), channel_id=1, source_target_pairs={{1,0},{5,4},{9,8}} | collective-permute-start | bytes 3145736 | tf_op jit(solution)/shard_map/ppermute | solution.py:104
  493.7 43.2 %collective-permute-start.58 = (f32[512,512]{0,1:T(8,128)}, f32[512,512]{0,1:T(8,128)}, u32[]{:S(2)}, u32[]{:S(2)}) collective-permute-start(f32[512,512]{0,1:T(8,128)} %collective-permute-done.57), channel_id=1, source_target_pairs={{1,0}} | collective-permute-start | bytes 3145736 | tf_op jit(solution)/shard_map/ppermute | solution.py:104
  543.0 38.7 %collective-permute-start.56 = (f32[512,512]{0,1:T(8,128)}, f32[512,512]{0,1:T(8,128)}, u32[]{:S(2)}, u32[]{:S(2)}) collective-permute-start(f32[512,512]{0,1:T(8,128)} %get-tuple-element.7), channel_id=1, source_target_pairs={{4,0},{5,1}} | collective-permute-start | bytes 3145736 | tf_op jit(solution)/shard_map/ppermute | solution.py:104
  (87 other events, 457.0 us)
